TPU v7x, 512 devices: a whole 4x4x16 slice. The times are simulated.
512 devices in a mesh: rx: 32 (over z_lo, x), tx: 16 (over y, z_hi, core).
Axes of the slice: x: 4, y: 4, z: 16 (z_hi: 2, z_lo: 8; z = z_hi * 8 + z_lo), core: 2. Of those that a mesh axis runs over, the one named last changes fastest.
Arguments:
- sender_xy: int32 [2, 32768], P(None, ('tx', 'rx')), may hold values from 0 to 255, as said below
- listener_xy: int32 [2, 32768], P(None, ('rx', 'tx')), may hold values from 0 to 256, as said below
- powers: float32 [32768, 128], P(('tx', 'rx')), may hold values from 0.25 to 1
- weight: int32 [32768], P(('rx', 'tx')), may hold values from 1 to 16
- fairness: int32 [32768], P(('rx', 'tx')), may hold values from 0 to 2
- step_code: int32 [1], replicated, may hold values from 256 to 4096
Outputs:
- quality: float32 [32768, 128], P(('rx', 'tx'))
- gradient: float32 [32768, 128], P(('tx', 'rx'))
- new_power: float32 [32768, 128], P(('tx', 'rx'))
- duality_gap: float32 [1], replicated
Inputs may be any that keep to these rules, and one draw needn't show every extreme that they name: `sender_xy`: row 0 lies in 0 to 255 and row 1 in 0 to 255. `listener_xy`: each entry equals the sender_xy entry of the same user or exceeds it by one.
All inputs are finite; a program needn't handle non-finite values.
Results may differ from a plain program's by a relative error of at most 0.0003.
Values sent between devices are 32-bit elements; how exact they have to be, the bound alone decides.
No kernel may reach another device: no remote copies, remote signals or barrier semaphores. Data moves between devices by JAX's collectives and lax.ppermute only.
A program may use at most 64 MiB of HBM per device.

v0:
```python
import jax
import jax.numpy as jnp
from jax import lax
from jax.sharding import PartitionSpec as P

NOISE_POWER = 0.05
ARRAY_GAIN = 32.0
WEIGHT_UNIT = 1.0 / 16.0
PEAK_POWER = 1.0


def path_gain(listen, sender):
    delta_x = listen[0].astype(jnp.float32)[:, None] - sender[0].astype(jnp.float32)[None, :]
    delta_y = listen[1].astype(jnp.float32)[:, None] - sender[1].astype(jnp.float32)[None, :]
    return 1.0 / (1.0 + delta_x * delta_x + delta_y * delta_y)


def derivatives(interference, signal, user_weight, user_fair):
    denominator = NOISE_POWER + interference
    quality = signal / denominator
    user_scale = WEIGHT_UNIT * user_weight.astype(jnp.float32)
    marginal = (
        user_scale[:, None]
        * jnp.exp(-user_fair.astype(jnp.float32)[:, None] * jnp.log(quality))
        / denominator
    )
    return (quality, marginal, marginal * quality)


def per_device(sender_xy, listener_xy, powers, weight, fairness, step_code):
    rx_here = lax.axis_index("rx")
    tx_here = lax.axis_index("tx")
    user_rows = powers.shape[0]
    channels = powers.shape[1]
    senders, sender_power = (
        lax.all_gather(sender_xy, "rx", axis=1, tiled=True),
        lax.all_gather(powers, "rx", axis=0, tiled=True),
    )
    listeners = lax.all_gather(listener_xy, "tx", axis=1, tiled=True)
    rx_width = listeners.shape[1]
    tx_width = senders.shape[1]
    row_start = rx_here * rx_width
    col_start = tx_here * tx_width
    gain_tile = path_gain(listeners, senders)
    row_ids = row_start + jnp.arange(rx_width, dtype=jnp.int32)
    col_ids = col_start + jnp.arange(tx_width, dtype=jnp.int32)
    diagonal = row_ids[:, None] == col_ids[None, :]
    crossing = jnp.where(diagonal, 0.0, gain_tile)
    own_gain = jnp.sum(jnp.where(diagonal, gain_tile, 0.0), axis=1)
    offset = row_start % tx_width
    interference_part = jnp.dot(crossing, sender_power, precision=lax.Precision.HIGHEST)
    signal_part = (
        ARRAY_GAIN * own_gain[:, None] * lax.dynamic_slice_in_dim(sender_power, offset, rx_width, 0)
    )
    interference, signal = (
        lax.psum_scatter(interference_part, "tx", scatter_dimension=0, tiled=True),
        lax.psum_scatter(signal_part, "tx", scatter_dimension=0, tiled=True),
    )
    quality, marginal, pressure = derivatives(interference, signal, weight, fairness)
    marginal_all, pressure_all = (
        lax.all_gather(marginal, "tx", axis=0, tiled=True),
        lax.all_gather(pressure, "tx", axis=0, tiled=True),
    )
    own_term = ARRAY_GAIN * own_gain[:, None] * marginal_all
    own_full = lax.dynamic_update_slice_in_dim(
        jnp.zeros((tx_width, channels), jnp.float32), own_term, offset, 0
    )
    pushed = lax.dot_general(
        crossing, pressure_all, (((0,), (0,)), ((), ())), precision=lax.Precision.HIGHEST
    )
    totals = lax.psum(own_full - pushed, "rx")
    gradient = lax.dynamic_slice_in_dim(totals, rx_here * user_rows, user_rows, 0)
    target = PEAK_POWER * jax.nn.sigmoid(gradient)
    step_size = step_code[0].astype(jnp.float32) / 4096.0
    new_power = powers + step_size * (target - powers)
    gap_local = jnp.sum(PEAK_POWER * jnp.maximum(gradient, 0.0) - gradient * powers)
    gap_sum = lax.psum(gap_local, ("rx", "tx"))
    duality_gap = (
        gap_sum / (user_rows * channels * lax.axis_size("rx") * lax.axis_size("tx"))
    ).reshape(1)
    return (quality, gradient, new_power, duality_gap)


def solution(mesh):
    placed = (
        P(None, ("tx", "rx")),
        P(None, ("rx", "tx")),
        P(("tx", "rx"), None),
        P(("rx", "tx")),
        P(("rx", "tx")),
        P(),
    )
    return jax.shard_map(
        per_device,
        mesh=mesh,
        in_specs=placed,
        out_specs=(P(("rx", "tx"), None), P(("tx", "rx"), None), P(("tx", "rx"), None), P()),
        check_vma=False,
    )
```

profile of v0, /device:TPU:1, one launch (start us, length us, event | category | flops | bytes accessed | tf_op | source)
XLA Modules:
  0.0 1118.0 jit_solution(16016938262697707755)
XLA Ops:
  7.2 0.0 all-gather.4.cloned.1.call-start
  7.2 0.7 all-gather.4.cloned.1.call-update
  7.9 0.0 reduce-scatter.3.cloned.1.call-start
  8.0 51.2 %all-gather = s32[16,64,2]{1,2,0:T(2,128)S(1)} all-gather(s32[1,64,2]{1,2,0:T(2,128)} %bitcast.34), channel_id=1, replica_groups=mesh['rx'=32,'tx'=16] {'tx'}, dimensions={0}, use_global_device_ids=true | all-gather | bytes 8704 | tf_op jit(solution)/shard_map/all_gather | solution.py:39
  59.1 0.1 reshape.43
  59.3 104.0 %all-gather.1 = s32[32,64,2]{1,2,0:T(2,128)S(1)} all-gather(s32[1,64,2]{1,2,0:T(2,128)} %bitcast.35), channel_id=1, replica_groups=mesh['rx'=32,'tx'=16] {'rx'}, dimensions={0}, use_global_device_ids=true | all-gather | bytes 16896 | tf_op jit(solution)/shard_map/all_gather | solution.py:36
  163.3 0.1 reshape.45
  163.5 3.1 fusion
  166.5 49.7 %all-gather.4.cloned.1.call-done = f32[2048,128]{1,0:T(8,128)} async-done(((f32[64,128]{1,0:T(8,128)}), f32[2048,128]{1,0:T(8,128)}) %all-gather.4.cloned.1.call-update) | async-done | bytes 1048592 | tf_op jit(solution)/shard_map/all_gather | solution.py:37
  216.2 2.1 dynamic-slice_multiply_fusion
  218.4 0.0 reduce-scatter.3.cloned.1.call-update
  218.4 0.0 copy-start.3
  218.4 0.0 copy-start.4
  218.4 0.0 reduce-scatter.5.cloned.1.call-start
  218.5 9.3 fusion.2
  227.8 0.0 reduce-scatter.5.cloned.1.call-update
  227.8 0.0 all-reduce.2.cloned.1.call-start
  227.9 0.0 copy-done.3
  227.9 0.0 copy-done.4
  227.9 111.3 %reduce-scatter.3.cloned.1.call-done = f32[64,128]{1,0:T(8,128)} async-done(((f32[1024,128]{1,0:T(8,128)}), f32[64,128]{1,0:T(8,128)}) %reduce-scatter.3.cloned.1.call-update) | async-done | bytes 32784 | tf_op jit(solution)/shard_map/reduce_scatter | solution.py:57
  339.2 96.6 %reduce-scatter.5.cloned.1.call-done = f32[64,128]{1,0:T(8,128)} async-done(((f32[1024,128]{1,0:T(8,128)}), f32[64,128]{1,0:T(8,128)}) %reduce-scatter.5.cloned.1.call-update) | async-done | bytes 32784 | tf_op jit(solution)/shard_map/reduce_scatter | solution.py:56
  435.8 1.4 fusion.14
  437.2 43.2 %all_gather.18 = f32[1024,128]{1,0:T(8,128)S(1)} all-gather(f32[64,128]{1,0:T(8,128)S(1)} %get-tuple-element.7), channel_id=1, replica_groups=mesh['rx'=32,'tx'=16] {'tx'}, dimensions={0}, use_global_device_ids=true | all-gather | bytes 557056 | tf_op jit(solution)/shard_map/all_gather | solution.py:61
  480.4 49.4 %all_gather.19 = f32[1024,128]{1,0:T(8,128)S(1)} all-gather(f32[64,128]{1,0:T(8,128)S(1)} %get-tuple-element.6), channel_id=1, replica_groups=mesh['rx'=32,'tx'=16] {'tx'}, dimensions={0}, use_global_device_ids=true | all-gather | bytes 557056 | tf_op jit(solution)/shard_map/all_gather | solution.py:62
  529.7 0.1 broadcast_in_dim.7
  529.8 0.2 multiply_dynamic-update-slice_fusion
  530.0 16.3 %fusion.9 = f32[2048,128]{1,0:T(8,128)} fusion(f32[2048,128]{1,0:T(8,128)S(1)} %multiply_dynamic-update-slice_fusion, f32[1024,128]{1,0:T(8,128)S(1)} %all_gather.19, f32[2048]{0:T(1024)S(1)} %bitcast.27, f32[1024]{0:T(1024)S(1)} %bitcast.33, f32[2048]{0:T(1024)S(1)} %bitcast.24, f32[1024]{0:T(1024)S(1)} %bitcast.30, s32[2048]{0:T(1024)S(1)} %iota_add_fusion, ...), kind=kOutput, calls=%fused_computation.12 | convolution fusion | flops 3240361984 | bytes 2658304 | tf_op jit(solution)/shard_map/dot_general | solution.py:68
  546.3 0.0 all-reduce.2.cloned.1.call-update
  547.0 437.2 %all-reduce.2.cloned.1.call-done = f32[2048,128]{1,0:T(8,128)} async-done(((f32[2048,128]{1,0:T(8,128)}), f32[2048,128]{1,0:T(8,128)}) %all-reduce.2.cloned.1.call-update) | async-done | bytes 1048592 | tf_op jit(solution)/shard_map/psum | solution.py:71
  984.1 1.4 subtract_reduce_fusion
  985.5 123.6 %psum.15 = f32[]{:T(128)} all-reduce(f32[]{:T(128)} %get-tuple-element.4), channel_id=1, replica_groups=mesh['rx'=32,'tx'=16] {'rx','tx'}, use_global_device_ids=true, to_apply=%region_5.6 | all-reduce | flops 1 | bytes 8 | tf_op jit(solution)/shard_map/psum | solution.py:77
  1109.1 0.6 multiply_add_fusion
  (14 shorter events, 0.1 us)
Async XLA Ops:
  7.2 209.1 %all-gather.4.cloned.1.call-start = ((), (), s32[]{:S(2)}) async-start(), calls=%async_computation.2 | async-start | bytes 1081344 | tf_op jit(solution)/shard_map/all_gather | solution.py:37
  7.9 331.3 %reduce-scatter.3.cloned.1.call-start = ((), (), s32[]{:S(2)}) async-start(), calls=%async_computation.3 | async-start | bytes 557056 | tf_op jit(solution)/shard_map/reduce_scatter | solution.py:57
  216.2 2.2 copy-start.1
  218.4 9.5 copy-start.3
  218.4 9.5 copy-start.4
  218.4 217.4 %reduce-scatter.5.cloned.1.call-start = ((), (), s32[]{:S(2)}) async-start(), calls=%async_computation.4 | async-start | bytes 557056 | tf_op jit(solution)/shard_map/reduce_scatter | solution.py:56
  227.8 756.3 %all-reduce.2.cloned.1.call-start = ((), (), s32[]{:S(2)}) async-start(), calls=%async_computation.5 | async-start | bytes 2097152 | tf_op jit(solution)/shard_map/psum | solution.py:71
  546.3 437.8 %copy-start = (f32[64,128]{1,0:T(8,128)S(1)}, f32[64,128]{1,0:T(8,128)}, u32[]{:S(2)}) copy-start(f32[64,128]{1,0:T(8,128)} %param.8) | copy-start | bytes 98308
  985.5 124.9 %copy-start.2 = (f32[64,128]{1,0:T(8,128)}, f32[64,128]{1,0:T(8,128)S(1)}, u32[]{:S(2)}) copy-start(f32[64,128]{1,0:T(8,128)S(1)} %get-tuple-element.5) | copy-start | bytes 98308
Sparse Core Ops, SparseCore 0:
  10.1 206.1 all-gather.3
  220.9 118.3 reduce-scatter.2
  344.6 91.1 reduce-scatter.4
  546.4 437.6 all-reduce.1
where the time goes:
time: 1120 us
  waiting for transfers between devices  695 us (62%)
  blocking collectives  371 us (33%)
  matrix products  25.6 us (2%)
  between operations  16.3 us (1%)
    psum x1, waiting for transfers between devices, per_device(): totals = lax.psum(own_full - pushed, 'rx')  437 us
    psum x1, blocking collectives, per_device(): gap_sum = lax.psum(gap_local, ('rx', 'tx'))  124 us
    reduce_scatter x1, waiting for transfers between devices, per_device(): lax.psum_scatter(signal_part, 'tx', scatter_dimension=0, tiled=True)  111 us
    all_gather x1, blocking collectives, per_device(): lax.all_gather(sender_xy, 'rx', axis=1, tiled=True)  104 us
    reduce_scatter x1, waiting for transfers between devices, per_device(): lax.psum_scatter(interference_part, 'tx', scatter_dimension=0, tiled=True)  96.6 us
    all_gather x1, blocking collectives, per_device(): listeners = lax.all_gather(listener_xy, 'tx', axis=1, tiled=True)  51.2 us
    all_gather x1, waiting for transfers between devices, per_device(): lax.all_gather(powers, 'rx', axis=0, tiled=True)  49.7 us
    all_gather x1, blocking collectives, per_device(): lax.all_gather(pressure, 'tx', axis=0, tiled=True)  49.4 us
  transfers between devices with their start and end apart: 4, of which 4 were waited for; matrix products, arithmetic and copies ran while one was open for 1% of the time, Pallas kernels for 0%

commit v1 on v0

--- a/solution.py
+++ b/solution.py
@@ -68,7 +68,7 @@
     pushed = lax.dot_general(
         crossing, pressure_all, (((0,), (0,)), ((), ())), precision=lax.Precision.HIGHEST
     )
-    totals = lax.psum(own_full - pushed, "rx")
+    totals = jnp.sum(lax.all_gather(own_full - pushed, "rx"), axis=0)
     gradient = lax.dynamic_slice_in_dim(totals, rx_here * user_rows, user_rows, 0)
     target = PEAK_POWER * jax.nn.sigmoid(gradient)
     step_size = step_code[0].astype(jnp.float32) / 4096.0

time: 1120 us -> 1060 us (0.946)
  waiting for transfers between devices: 695 us -> 618 us
    psum x1 -> x0, waiting for transfers between devices: 437 us -> none  [per_device(): totals = lax.psum(own_full - pushed, 'rx')]
    all_gather x0 -> x1, waiting for transfers between devices: none -> 367 us  [per_device(): totals = jnp.sum(lax.all_gather(own_full - pushed, 'rx'), axis=0)]
    psum x1, blocking collectives: 124 us -> 101 us  [per_device(): gap_sum = lax.psum(gap_local, ('rx', 'tx'))]
    reduce_scatter x1, waiting for transfers between devices: 96.6 us -> 114 us  [per_device(): lax.psum_scatter(interference_part, 'tx', scatter_dimension=0, tiled=True)]
    all_gather x1, blocking collectives: 49.4 us -> 64.4 us  [per_device(): lax.all_gather(pressure, 'tx', axis=0, tiled=True)]
    reduce_scatter x1, waiting for transfers between devices: 111 us -> 96.6 us  [per_device(): lax.psum_scatter(signal_part, 'tx', scatter_dimension=0, tiled=True)]
    reduce_sum x0 -> x1, other arithmetic: none -> 11.7 us  [per_device(): totals = jnp.sum(lax.all_gather(own_full - pushed, 'rx'), axis=0)]
  transfers between devices with their start and end apart: 4 -> 4, of which waited for: 4 -> 4; matrix products, arithmetic and copies ran while one was open for 1% -> 0% of each run, Pallas kernels for 0% -> 0%
where the time goes in v1:
time: 1060 us
  waiting for transfers between devices  618 us (58%)
  blocking collectives  377 us (36%)
  matrix products  26.9 us (3%)
  other arithmetic  18.7 us (2%)
  between operations  16.3 us (2%)
    all_gather x1, waiting for transfers between devices, per_device(): totals = jnp.sum(lax.all_gather(own_full - pushed, 'rx'), axis=0)  367 us
    reduce_scatter x1, waiting for transfers between devices, per_device(): lax.psum_scatter(interference_part, 'tx', scatter_dimension=0, tiled=True)  114 us
    all_gather x1, blocking collectives, per_device(): lax.all_gather(sender_xy, 'rx', axis=1, tiled=True)  112 us
    psum x1, blocking collectives, per_device(): gap_sum = lax.psum(gap_local, ('rx', 'tx'))  101 us
    reduce_scatter x1, waiting for transfers between devices, per_device(): lax.psum_scatter(signal_part, 'tx', scatter_dimension=0, tiled=True)  96.6 us
    all_gather x1, blocking collectives, per_device(): lax.all_gather(pressure, 'tx', axis=0, tiled=True)  64.4 us
    all_gather x1, blocking collectives, per_device(): listeners = lax.all_gather(listener_xy, 'tx', axis=1, tiled=True)  56.4 us
    all_gather x1, blocking collectives, per_device(): lax.all_gather(marginal, 'tx', axis=0, tiled=True)  42.6 us
  transfers between devices with their start and end apart: 4, of which 4 were waited for; matrix products, arithmetic and copies ran while one was open for 0% of the time, Pallas kernels for 0%

profile of v1, /device:TPU:1, one launch (start us, length us, event | category | flops | bytes accessed | tf_op | source)
XLA Modules:
  0.0 1057.1 jit_solution(4130639457008122297)
XLA Ops:
  7.2 0.0 all-gather.6.cloned.1.call-start
  7.2 0.7 all-gather.6.cloned.1.call-update
  7.9 0.0 reduce-scatter.5.cloned.1.call-start
  7.9 112.2 %all-gather.2 = s32[32,64,2]{1,2,0:T(2,128)S(1)} all-gather(s32[1,64,2]{1,2,0:T(2,128)} %bitcast.36), channel_id=1, replica_groups=mesh['rx'=32,'tx'=16] {'rx'}, dimensions={0}, use_global_device_ids=true | all-gather | bytes 16896 | tf_op jit(solution)/shard_map/all_gather | solution.py:36
  120.2 0.1 reshape.46
  120.3 56.4 %all-gather.1 = s32[16,64,2]{1,2,0:T(2,128)S(1)} all-gather(s32[1,64,2]{1,2,0:T(2,128)} %bitcast.37), channel_id=1, replica_groups=mesh['rx'=32,'tx'=16] {'tx'}, dimensions={0}, use_global_device_ids=true | all-gather | bytes 8704 | tf_op jit(solution)/shard_map/all_gather | solution.py:39
  176.7 0.1 reshape.44
  176.8 39.9 %all-gather.6.cloned.1.call-done = f32[2048,128]{1,0:T(8,128)} async-done(((f32[64,128]{1,0:T(8,128)}), f32[2048,128]{1,0:T(8,128)}) %all-gather.6.cloned.1.call-update) | async-done | bytes 1048592 | tf_op jit(solution)/shard_map/all_gather | solution.py:37
  216.7 10.6 %fusion.2 = f32[1024,128]{1,0:T(8,128)} fusion(f32[2048,128]{1,0:T(8,128)} %all-gather.6.cloned.1.call-done, f32[2048]{0:T(1024)S(1)} %bitcast.27, f32[1024]{0:T(1024)S(1)} %bitcast.33, f32[2048]{0:T(1024)S(1)} %bitcast.24, f32[1024]{0:T(1024)S(1)} %bitcast.30, s32[2048]{0:T(1024)S(1)} %iota_add_fusion, s32[1024]{0:T(1024)S(1)} %iota_add_fusion.1), kind=kOutput, calls=%fused_computation.5 | convolution fusion | flops 3240099840 | bytes 1609728 | tf_op jit(solution)/shard_map/dot_general | solution.py:51
  227.4 0.0 reduce-scatter.5.cloned.1.call-update
  227.4 0.0 reduce-scatter.3.cloned.1.call-start
  227.5 3.1 fusion
  230.6 0.0 copy-done.1
  230.6 1.0 dynamic-slice_multiply_fusion
  231.6 0.0 reduce-scatter.3.cloned.1.call-update
  231.6 0.0 all-gather.8.cloned.1.call-start
  231.7 0.0 copy-done.3
  231.7 113.7 %reduce-scatter.5.cloned.1.call-done = f32[64,128]{1,0:T(8,128)} async-done(((f32[1024,128]{1,0:T(8,128)}), f32[64,128]{1,0:T(8,128)}) %reduce-scatter.5.cloned.1.call-update) | async-done | bytes 32784 | tf_op jit(solution)/shard_map/reduce_scatter | solution.py:56
  345.4 96.6 %reduce-scatter.3.cloned.1.call-done = f32[64,128]{1,0:T(8,128)} async-done(((f32[1024,128]{1,0:T(8,128)}), f32[64,128]{1,0:T(8,128)}) %reduce-scatter.3.cloned.1.call-update) | async-done | bytes 32784 | tf_op jit(solution)/shard_map/reduce_scatter | solution.py:57
  442.0 1.4 fusion.14
  443.4 42.6 %all_gather.24 = f32[1024,128]{1,0:T(8,128)S(1)} all-gather(f32[64,128]{1,0:T(8,128)S(1)} %get-tuple-element.7), channel_id=1, replica_groups=mesh['rx'=32,'tx'=16] {'tx'}, dimensions={0}, use_global_device_ids=true | all-gather | bytes 557056 | tf_op jit(solution)/shard_map/all_gather | solution.py:61
  486.0 64.4 %all_gather.25 = f32[1024,128]{1,0:T(8,128)S(1)} all-gather(f32[64,128]{1,0:T(8,128)S(1)} %get-tuple-element.6), channel_id=1, replica_groups=mesh['rx'=32,'tx'=16] {'tx'}, dimensions={0}, use_global_device_ids=true | all-gather | bytes 557056 | tf_op jit(solution)/shard_map/all_gather | solution.py:62
  550.4 0.1 broadcast_in_dim.7
  550.5 0.2 multiply_dynamic-update-slice_fusion
  550.7 16.2 %fusion.9 = f32[2048,128]{1,0:T(8,128)} fusion(f32[2048,128]{1,0:T(8,128)S(1)} %multiply_dynamic-update-slice_fusion, f32[1024,128]{1,0:T(8,128)S(1)} %all_gather.25, f32[2048]{0:T(1024)S(1)} %bitcast.29, f32[1024]{0:T(1024)S(1)} %bitcast.35, f32[2048]{0:T(1024)S(1)} %bitcast.26, f32[1024]{0:T(1024)S(1)} %bitcast.32, s32[2048]{0:T(1024)S(1)} %iota_add_fusion, ...), kind=kOutput, calls=%fused_computation.12 | convolution fusion | flops 3240361984 | bytes 2658304 | tf_op jit(solution)/shard_map/dot_general | solution.py:68
  567.0 0.0 all-gather.8.cloned.1.call-update
  567.6 367.2 %all-gather.8.cloned.1.call-done = f32[65536,128]{1,0:T(8,128)} async-done(((f32[2048,128]{1,0:T(8,128)}), f32[65536,128]{1,0:T(8,128)}) %all-gather.8.cloned.1.call-update) | async-done | bytes 33554448 | tf_op jit(solution)/shard_map/all_gather | solution.py:71
  934.9 11.7 %reduce_sum.28 = f32[2048,128]{1,0:T(8,128)S(1)} reduce(f32[32,2048,128]{2,1,0:T(8,128)} %bitcast.21, f32[]{:T(128)} %constant.38.clone.1), dimensions={0}, to_apply=%region_3.4 | reduce | flops 8126464 | bytes 34603012 | tf_op jit(solution)/shard_map/reduce_sum | solution.py:71
  946.6 0.6 subtract_reduce_fusion
  947.2 100.9 %psum.7 = f32[]{:T(128)} all-reduce(f32[]{:T(128)} %get-tuple-element.4), channel_id=1, replica_groups=mesh['rx'=32,'tx'=16] {'rx','tx'}, use_global_device_ids=true, to_apply=%region_5.6 | all-reduce | flops 1 | bytes 8 | tf_op jit(solution)/shard_map/psum | solution.py:77
  1048.1 0.6 multiply_add_fusion
  1049.4 0.0 copy-done.2
  (15 shorter events, 0.1 us)
Async XLA Ops:
  7.2 209.6 %all-gather.6.cloned.1.call-start = ((), (), s32[]{:S(2)}) async-start(), calls=%async_computation.2 | async-start | bytes 1081344 | tf_op jit(solution)/shard_map/all_gather | solution.py:37
  7.9 337.5 %reduce-scatter.5.cloned.1.call-start = ((), (), s32[]{:S(2)}) async-start(), calls=%async_computation.4 | async-start | bytes 557056 | tf_op jit(solution)/shard_map/reduce_scatter | solution.py:56
  216.7 13.8 %copy-start.1 = (f32[2048,128]{1,0:T(8,128)S(1)}, f32[2048,128]{1,0:T(8,128)}, u32[]{:S(2)}) copy-start(f32[2048,128]{1,0:T(8,128)} %all-gather.6.cloned.1.call-done) | copy-start | bytes 3145732
  216.7 14.9 %copy-start.3 = (s32[64]{0:T(128)S(1)}, s32[64]{0:T(128)}, u32[]{:S(2)}) copy-start(s32[64]{0:T(128)} %param.10) | copy-start | bytes 772
  216.7 14.9 %copy-start.4 = (s32[64]{0:T(128)S(1)}, s32[64]{0:T(128)}, u32[]{:S(2)}) copy-start(s32[64]{0:T(128)} %param.9) | copy-start | bytes 772
  227.4 214.6 %reduce-scatter.3.cloned.1.call-start = ((), (), s32[]{:S(2)}) async-start(), calls=%async_computation.3 | async-start | bytes 557056 | tf_op jit(solution)/shard_map/reduce_scatter | solution.py:57
  231.6 703.3 %all-gather.8.cloned.1.call-start = ((), (), s32[]{:S(2)}) async-start(), calls=%async_computation.5 | async-start | bytes 34603008 | tf_op jit(solution)/shard_map/all_gather | solution.py:71
  934.9 11.7 %copy-start = (f32[64,128]{1,0:T(8,128)S(1)}, f32[64,128]{1,0:T(8,128)}, u32[]{:S(2)}) copy-start(f32[64,128]{1,0:T(8,128)} %param.8) | copy-start | bytes 98308
  947.2 102.2 %copy-start.2 = (f32[64,128]{1,0:T(8,128)}, f32[64,128]{1,0:T(8,128)S(1)}, u32[]{:S(2)}) copy-start(f32[64,128]{1,0:T(8,128)S(1)} %get-tuple-element.5) | copy-start | bytes 98308
Sparse Core Ops, SparseCore 0:
  10.1 206.6 all-gather.5
  227.5 117.8 reduce-scatter.4
  350.8 91.2 reduce-scatter.2
  567.1 367.7 all-gather.7
